TPU v7x, 512 devices: a whole 4x8x8 slice. The times are simulated.
512 devices in a mesh: region: 16 (over y, core), local: 32 (over z, x).
Axes of the slice: x: 4, y: 8, z: 8, core: 2. Of those that a mesh axis runs over, the one named last changes fastest.
Arguments:
- positions: float32 [32768, 4, 256], P(('region', 'local')), as said below
- pair_list: int32 [32768, 2], P(('region', 'local')), may hold values from 0 to 639, as said below
- pair_count: int32 [512], P(('region', 'local')), may hold values from 16 to 64, as said below
- active: int32 [32768], P(('region', 'local')), may hold values 0 or 1
Outputs:
- accel: float32 [32768, 3, 256], P(('region', 'local'))
Inputs may be any that keep to these rules, and one draw needn't show every extreme that they name: `pair_list`: column 0 lies in 0 to 63 and column 1 in 0 to 639; no slot pairs a leaf with itself. `pair_count`: whole region groups carry the full 64 live slots on every device, two to four times the count of other groups' devices. `positions`: masses are positive.
All inputs are finite; a program needn't handle non-finite values. No bound on the sum of `active` on one device may be relied on, other than what follows from the above.
Results may differ from a plain program's by a relative error of at most 0.0003.
Values sent between devices are 32-bit elements; how exact they have to be, the bound alone decides.
A program may use at most 64 MiB of HBM per device.

v0:
```python
import math

import jax
import jax.numpy as jnp
from jax import lax
from jax.sharding import PartitionSpec as P


def passed_along(value, axis, steps):
    count = lax.axis_size(axis)
    pairs = [(source, (source + steps) % count) for source in range(count)]
    return lax.ppermute(value, axis, pairs)


def pair_kernel(first, second):
    dx = second[:3, None, :] - first[:3, :, None]
    r2 = jnp.sum(dx * dx, axis=0) + 0.09
    dist = jnp.sqrt(r2)
    kern = (lax.erfc(dist * 0.5) + dist * (1.0 / math.sqrt(math.pi)) * jnp.exp(-r2 * 0.25)) / (
        r2 * dist
    )
    weighted = dx * kern[None, :, :]
    on_first = jnp.sum(weighted * second[3][None, None, :], axis=2)
    on_second = -jnp.sum(weighted * first[3][None, :, None], axis=1)
    return (on_first, on_second)


def own_window(positions):
    pieces = {}
    for offset in (-2, -1, 1, 2):
        pieces[offset] = passed_along(positions, "local", -offset)
    pieces[0] = positions
    return jnp.concatenate([pieces[offset] for offset in (-2, -1, 0, 1, 2)], axis=0)


def return_own(reaction, leaf_dev):
    total = reaction[2 * leaf_dev : 3 * leaf_dev]
    for offset in (-2, -1, 1, 2):
        piece = reaction[(offset + 2) * leaf_dev : (offset + 3) * leaf_dev]
        total = total + passed_along(piece, "local", offset)
    return total


def shards(positions, pair_list, pair_count, active):
    leaf_dev = positions.shape[0]
    width = positions.shape[2]
    here_window = own_window(positions)
    next_region = passed_along(here_window, "region", -1)
    table = jnp.concatenate([here_window, next_region], axis=0)
    span = here_window.shape[0]
    slots = pair_list.shape[0]
    alive = (jnp.arange(slots, dtype=jnp.int32) < pair_count[0]).astype(jnp.float32)
    grouped = pair_list.reshape(slots // 4, 4, 2)
    alive = alive.reshape(slots // 4, 4)
    own_acc = jnp.zeros((leaf_dev, 3, width), jnp.float32)
    reaction = jnp.zeros((2 * span, 3, width), jnp.float32)

    def step(carry, inputs):
        own_part, react_part = carry
        pairs, weight = inputs
        first = positions[pairs[:, 0]]
        second = table[pairs[:, 1]]
        on_first, on_second = jax.vmap(pair_kernel)(first, second)
        scale = weight[:, None, None]
        own_part = own_part.at[pairs[:, 0]].add(on_first * scale)
        react_part = react_part.at[pairs[:, 1]].add(on_second * scale)
        return ((own_part, react_part), None)

    (own_acc, reaction), unused = lax.scan(step, (own_acc, reaction), (grouped, alive))
    react_here = reaction[:span]
    react_next = reaction[span:]
    arrived = passed_along(react_next, "region", 1)
    share = return_own(react_here + arrived, leaf_dev)
    return (own_acc + share) * active.astype(jnp.float32)[:, None, None]


def solution(mesh):
    return jax.shard_map(
        shards,
        mesh=mesh,
        in_specs=(
            P(("region", "local"), None, None),
            P(("region", "local"), None),
            P(("region", "local")),
            P(("region", "local")),
        ),
        out_specs=P(("region", "local"), None, None),
        check_vma=False,
    )
```

profile of v0, /device:TPU:2, one launch (start us, length us, event | category | flops | bytes accessed | tf_op | source)
XLA Modules:
  0.0 248.0 jit_solution(6729832999506487608)
XLA Ops:
  0.0 4.2 %collective-permute-start = (f32[64,4,256]{2,1,0:T(4,128)}, f32[64,4,256]{2,1,0:T(4,128)S(1)}, u32[]{:S(2)}, u32[]{:S(2)}) collective-permute-start(f32[64,4,256]{2,1,0:T(4,128)} %param.6), channel_id=1, source_target_pairs={{0,2},{1,3},{2,4},{3,5},{4,6},{5,7},{6,8},{7,9},{8,10},{9,11},{10,... | collective-permute-start | bytes 786440 | tf_op jit(solution)/shard_map/ppermute | solution.py:12
  4.2 3.6 %collective-permute-start.1 = (f32[64,4,256]{2,1,0:T(4,128)}, f32[64,4,256]{2,1,0:T(4,128)S(1)}, u32[]{:S(2)}, u32[]{:S(2)}) collective-permute-start(f32[64,4,256]{2,1,0:T(4,128)} %param.6), channel_id=1, source_target_pairs={{0,1},{1,2},{2,3},{3,4},{4,5},{5,6},{6,7},{7,8},{8,9},{9,10},{10,1... | collective-permute-start | bytes 786440 | tf_op jit(solution)/shard_map/ppermute | solution.py:12
  7.8 4.0 %collective-permute-start.2 = (f32[64,4,256]{2,1,0:T(4,128)}, f32[64,4,256]{2,1,0:T(4,128)S(1)}, u32[]{:S(2)}, u32[]{:S(2)}) collective-permute-start(f32[64,4,256]{2,1,0:T(4,128)} %param.6), channel_id=1, source_target_pairs={{0,31},{1,0},{2,1},{3,2},{4,3},{5,4},{6,5},{7,6},{8,7},{9,8},{10,9... | collective-permute-start | bytes 786440 | tf_op jit(solution)/shard_map/ppermute | solution.py:12
  11.8 8.6 %collective-permute-start.3 = (f32[64,4,256]{2,1,0:T(4,128)}, f32[64,4,256]{2,1,0:T(4,128)S(1)}, u32[]{:S(2)}, u32[]{:S(2)}) collective-permute-start(f32[64,4,256]{2,1,0:T(4,128)} %param.6), channel_id=1, source_target_pairs={{0,30},{1,31},{2,0},{3,1},{4,2},{5,3},{6,4},{7,5},{8,6},{9,7},{10,... | collective-permute-start | bytes 786440 | tf_op jit(solution)/shard_map/ppermute | solution.py:12
  23.4 6.9 %collective-permute-done.3 = f32[64,4,256]{2,1,0:T(4,128)S(1)} collective-permute-done((f32[64,4,256]{2,1,0:T(4,128)}, f32[64,4,256]{2,1,0:T(4,128)S(1)}, u32[]{:S(2)}, u32[]{:S(2)}) %collective-permute-start.3) | collective-permute-done | bytes 262176 | tf_op jit(solution)/shard_map/ppermute | solution.py:12
  32.0 3.1 %collective-permute-start.4 = (f32[320,4,256]{2,1,0:T(4,128)S(1)}, f32[320,4,256]{2,1,0:T(4,128)S(1)}, u32[]{:S(2)}, u32[]{:S(2)}) collective-permute-start(f32[320,4,256]{2,1,0:T(4,128)S(1)} %get-tuple-element.92), channel_id=1, source_target_pairs={{0,480},{32,0},{64,32},{96,64},{128,96},{160,128},{192,160},{224,1... | collective-permute-start | bytes 3932168 | tf_op jit(solution)/shard_map/ppermute | solution.py:12
  35.8 14.4 %collective-permute-done.4 = f32[320,4,256]{2,1,0:T(4,128)S(1)} collective-permute-done((f32[320,4,256]{2,1,0:T(4,128)S(1)}, f32[320,4,256]{2,1,0:T(4,128)S(1)}, u32[]{:S(2)}, u32[]{:S(2)}) %collective-permute-start.4) | collective-permute-done | bytes 1310752 | tf_op jit(solution)/shard_map/ppermute | solution.py:12
  51.9 157.4 %while.12 = (s32[]{:T(128)}, f32[64,3,256]{2,1,0:T(4,128)S(1)}, f32[640,3,256]{2,1,0:T(4,128)S(1)}, s32[16,4,2]{1,0,2:T(8,128)S(1)}, f32[640,4,256]{2,1,0:T(4,12...) while((s32[]{:T(128)}, f32[64,3,256]{2,1,0:T(4,128)S(1)}, f32[640,3,256]{2,1,0:T(4,128)S(1)}, ...), condition=%wide.region_6.7_spmd, body=%wide.region_0.6_spmd.sunk | while | flops 24914968 | bytes 4505965 | solution.py:69
  56.2 2.8 %fusion.34 = f32[4,256,256]{2,1,0:T(8,128)S(1)} fusion(f32[4,256,256]{2,1,0:T(8,128)S(1)} %fusion.33), kind=kLoop, calls=%fused_computation.17.clone.1 | loop fusion | flops 18087936 | bytes 2097152 | tf_op jit(solution)/shard_map/while/body/eval_jaxpr/vmap()/div | solution.py:19
  66.1 2.8 %fusion.34 = f32[4,256,256]{2,1,0:T(8,128)S(1)} fusion(f32[4,256,256]{2,1,0:T(8,128)S(1)} %fusion.33), kind=kLoop, calls=%fused_computation.17.clone.1 | loop fusion | flops 18087936 | bytes 2097152 | tf_op jit(solution)/shard_map/while/body/eval_jaxpr/vmap()/div | solution.py:19
  75.9 2.8 %fusion.34 = f32[4,256,256]{2,1,0:T(8,128)S(1)} fusion(f32[4,256,256]{2,1,0:T(8,128)S(1)} %fusion.33), kind=kLoop, calls=%fused_computation.17.clone.1 | loop fusion | flops 18087936 | bytes 2097152 | tf_op jit(solution)/shard_map/while/body/eval_jaxpr/vmap()/div | solution.py:19
  85.8 2.8 %fusion.34 = f32[4,256,256]{2,1,0:T(8,128)S(1)} fusion(f32[4,256,256]{2,1,0:T(8,128)S(1)} %fusion.33), kind=kLoop, calls=%fused_computation.17.clone.1 | loop fusion | flops 18087936 | bytes 2097152 | tf_op jit(solution)/shard_map/while/body/eval_jaxpr/vmap()/div | solution.py:19
  95.6 2.8 %fusion.34 = f32[4,256,256]{2,1,0:T(8,128)S(1)} fusion(f32[4,256,256]{2,1,0:T(8,128)S(1)} %fusion.33), kind=kLoop, calls=%fused_computation.17.clone.1 | loop fusion | flops 18087936 | bytes 2097152 | tf_op jit(solution)/shard_map/while/body/eval_jaxpr/vmap()/div | solution.py:19
  105.4 2.8 %fusion.34 = f32[4,256,256]{2,1,0:T(8,128)S(1)} fusion(f32[4,256,256]{2,1,0:T(8,128)S(1)} %fusion.33), kind=kLoop, calls=%fused_computation.17.clone.1 | loop fusion | flops 18087936 | bytes 2097152 | tf_op jit(solution)/shard_map/while/body/eval_jaxpr/vmap()/div | solution.py:19
  115.3 2.8 %fusion.34 = f32[4,256,256]{2,1,0:T(8,128)S(1)} fusion(f32[4,256,256]{2,1,0:T(8,128)S(1)} %fusion.33), kind=kLoop, calls=%fused_computation.17.clone.1 | loop fusion | flops 18087936 | bytes 2097152 | tf_op jit(solution)/shard_map/while/body/eval_jaxpr/vmap()/div | solution.py:19
  125.1 2.8 %fusion.34 = f32[4,256,256]{2,1,0:T(8,128)S(1)} fusion(f32[4,256,256]{2,1,0:T(8,128)S(1)} %fusion.33), kind=kLoop, calls=%fused_computation.17.clone.1 | loop fusion | flops 18087936 | bytes 2097152 | tf_op jit(solution)/shard_map/while/body/eval_jaxpr/vmap()/div | solution.py:19
  134.9 2.8 %fusion.34 = f32[4,256,256]{2,1,0:T(8,128)S(1)} fusion(f32[4,256,256]{2,1,0:T(8,128)S(1)} %fusion.33), kind=kLoop, calls=%fused_computation.17.clone.1 | loop fusion | flops 18087936 | bytes 2097152 | tf_op jit(solution)/shard_map/while/body/eval_jaxpr/vmap()/div | solution.py:19
  154.6 2.8 %fusion.34 = f32[4,256,256]{2,1,0:T(8,128)S(1)} fusion(f32[4,256,256]{2,1,0:T(8,128)S(1)} %fusion.33), kind=kLoop, calls=%fused_computation.17.clone.1 | loop fusion | flops 18087936 | bytes 2097152 | tf_op jit(solution)/shard_map/while/body/eval_jaxpr/vmap()/div | solution.py:19
  164.5 2.8 %fusion.34 = f32[4,256,256]{2,1,0:T(8,128)S(1)} fusion(f32[4,256,256]{2,1,0:T(8,128)S(1)} %fusion.33), kind=kLoop, calls=%fused_computation.17.clone.1 | loop fusion | flops 18087936 | bytes 2097152 | tf_op jit(solution)/shard_map/while/body/eval_jaxpr/vmap()/div | solution.py:19
  209.8 14.9 %collective-permute-done.5 = f32[320,3,256]{2,0,1:T(8,128)S(1)} collective-permute-done((f32[320,3,256]{2,0,1:T(8,128)S(1)}, f32[320,3,256]{2,0,1:T(8,128)S(1)}, u32[]{:S(2)}, u32[]{:S(2)}) %collective-permute-start.5) | collective-permute-done | bytes 983072 | tf_op jit(solution)/shard_map/ppermute | solution.py:12
  224.9 3.5 %collective-permute-start.6 = (f32[64,3,256]{2,0,1:T(8,128)S(1)}, f32[64,3,256]{2,0,1:T(8,128)S(1)}, u32[]{:S(2)}, u32[]{:S(2)}) collective-permute-start(f32[64,3,256]{2,0,1:T(8,128)S(1)} %get-tuple-element.88), channel_id=1, source_target_pairs={{0,30},{1,31},{2,0},{3,1},{4,2},{5,3},{6,4},{7,5},{8,6},{9,7},{10,... | collective-permute-start | bytes 589832 | tf_op jit(solution)/shard_map/ppermute | solution.py:12
  228.4 4.0 %collective-permute-start.7 = (f32[64,3,256]{2,0,1:T(8,128)S(1)}, f32[64,3,256]{2,0,1:T(8,128)S(1)}, u32[]{:S(2)}, u32[]{:S(2)}) collective-permute-start(f32[64,3,256]{2,0,1:T(8,128)S(1)} %get-tuple-element.91), channel_id=1, source_target_pairs={{0,31},{1,0},{2,1},{3,2},{4,3},{5,4},{6,5},{7,6},{8,7},{9,8},{10,9... | collective-permute-start | bytes 589832 | tf_op jit(solution)/shard_map/ppermute | solution.py:12
  234.4 5.8 %collective-permute-start.9 = (f32[64,3,256]{2,0,1:T(8,128)S(1)}, f32[64,3,256]{2,0,1:T(8,128)S(1)}, u32[]{:S(2)}, u32[]{:S(2)}) collective-permute-start(f32[64,3,256]{2,0,1:T(8,128)S(1)} %get-tuple-element.89), channel_id=1, source_target_pairs={{0,2},{1,3},{2,4},{3,5},{4,6},{5,7},{6,8},{7,9},{8,10},{9,11},{10,... | collective-permute-start | bytes 589832 | tf_op jit(solution)/shard_map/ppermute | solution.py:12
  240.9 6.3 %collective-permute-done.9 = f32[64,3,256]{2,0,1:T(8,128)S(1)} collective-permute-done((f32[64,3,256]{2,0,1:T(8,128)S(1)}, f32[64,3,256]{2,0,1:T(8,128)S(1)}, u32[]{:S(2)}, u32[]{:S(2)}) %collective-permute-start.9) | collective-permute-done | bytes 196640 | tf_op jit(solution)/shard_map/ppermute | solution.py:12
  (275 shorter events, 135.4 us)
Async XLA Ops:
  0.0 35.1 %copy-start.1 = (s32[64,2]{0,1:T(2,128)S(1)}, s32[64,2]{0,1:T(2,128)}, u32[]{:S(2)}) copy-start(s32[64,2]{0,1:T(2,128)} %param.7) | copy-start | bytes 1540
  0.0 20.4 %collective-permute-start = (f32[64,4,256]{2,1,0:T(4,128)}, f32[64,4,256]{2,1,0:T(4,128)S(1)}, u32[]{:S(2)}, u32[]{:S(2)}) collective-permute-start(f32[64,4,256]{2,1,0:T(4,128)} %param.6), channel_id=1, source_target_pairs={{0,2},{1,3},{2,4},{3,5},{4,6},{5,7},{6,8},{7,9},{8,10},{9,11},{10,... | collective-permute-start | bytes 786440 | tf_op jit(solution)/shard_map/ppermute | solution.py:12
  4.2 16.4 %collective-permute-start.1 = (f32[64,4,256]{2,1,0:T(4,128)}, f32[64,4,256]{2,1,0:T(4,128)S(1)}, u32[]{:S(2)}, u32[]{:S(2)}) collective-permute-start(f32[64,4,256]{2,1,0:T(4,128)} %param.6), channel_id=1, source_target_pairs={{0,1},{1,2},{2,3},{3,4},{4,5},{5,6},{6,7},{7,8},{8,9},{9,10},{10,1... | collective-permute-start | bytes 786440 | tf_op jit(solution)/shard_map/ppermute | solution.py:12
  7.8 15.6 %collective-permute-start.2 = (f32[64,4,256]{2,1,0:T(4,128)}, f32[64,4,256]{2,1,0:T(4,128)S(1)}, u32[]{:S(2)}, u32[]{:S(2)}) collective-permute-start(f32[64,4,256]{2,1,0:T(4,128)} %param.6), channel_id=1, source_target_pairs={{0,31},{1,0},{2,1},{3,2},{4,3},{5,4},{6,5},{7,6},{8,7},{9,8},{10,9... | collective-permute-start | bytes 786440 | tf_op jit(solution)/shard_map/ppermute | solution.py:12
  11.8 18.6 %collective-permute-start.3 = (f32[64,4,256]{2,1,0:T(4,128)}, f32[64,4,256]{2,1,0:T(4,128)S(1)}, u32[]{:S(2)}, u32[]{:S(2)}) collective-permute-start(f32[64,4,256]{2,1,0:T(4,128)} %param.6), channel_id=1, source_target_pairs={{0,30},{1,31},{2,0},{3,1},{4,2},{5,3},{6,4},{7,5},{8,6},{9,7},{10,... | collective-permute-start | bytes 786440 | tf_op jit(solution)/shard_map/ppermute | solution.py:12
  30.5 1.5 copy-start
  32.0 18.2 %collective-permute-start.4 = (f32[320,4,256]{2,1,0:T(4,128)S(1)}, f32[320,4,256]{2,1,0:T(4,128)S(1)}, u32[]{:S(2)}, u32[]{:S(2)}) collective-permute-start(f32[320,4,256]{2,1,0:T(4,128)S(1)} %get-tuple-element.92), channel_id=1, source_target_pairs={{0,480},{32,0},{64,32},{96,64},{128,96},{160,128},{192,160},{224,1... | collective-permute-start | bytes 3932168 | tf_op jit(solution)/shard_map/ppermute | solution.py:12
  209.7 30.5 %copy-start.2 = (s32[64]{0:T(128)S(1)}, s32[64]{0:T(128)}, u32[]{:S(2)}) copy-start(s32[64]{0:T(128)} %param.9) | copy-start | bytes 772
  209.7 14.9 %collective-permute-start.5 = (f32[320,3,256]{2,0,1:T(8,128)S(1)}, f32[320,3,256]{2,0,1:T(8,128)S(1)}, u32[]{:S(2)}, u32[]{:S(2)}) collective-permute-start(f32[320,3,256]{2,0,1:T(8,128)S(1)} %slice.57), channel_id=1, source_target_pairs={{0,32},{32,64},{64,96},{96,128},{128,160},{160,192},{192,224},{224... | collective-permute-start | bytes 2949128 | tf_op jit(solution)/shard_map/ppermute | solution.py:12
  224.9 15.4 %collective-permute-start.6 = (f32[64,3,256]{2,0,1:T(8,128)S(1)}, f32[64,3,256]{2,0,1:T(8,128)S(1)}, u32[]{:S(2)}, u32[]{:S(2)}) collective-permute-start(f32[64,3,256]{2,0,1:T(8,128)S(1)} %get-tuple-element.88), channel_id=1, source_target_pairs={{0,30},{1,31},{2,0},{3,1},{4,2},{5,3},{6,4},{7,5},{8,6},{9,7},{10,... | collective-permute-start | bytes 589832 | tf_op jit(solution)/shard_map/ppermute | solution.py:12
  228.4 11.8 %collective-permute-start.7 = (f32[64,3,256]{2,0,1:T(8,128)S(1)}, f32[64,3,256]{2,0,1:T(8,128)S(1)}, u32[]{:S(2)}, u32[]{:S(2)}) collective-permute-start(f32[64,3,256]{2,0,1:T(8,128)S(1)} %get-tuple-element.91), channel_id=1, source_target_pairs={{0,31},{1,0},{2,1},{3,2},{4,3},{5,4},{6,5},{7,6},{8,7},{9,8},{10,9... | collective-permute-start | bytes 589832 | tf_op jit(solution)/shard_map/ppermute | solution.py:12
  232.4 8.5 %collective-permute-start.8 = (f32[64,3,256]{2,0,1:T(8,128)S(1)}, f32[64,3,256]{2,0,1:T(8,128)S(1)}, u32[]{:S(2)}, u32[]{:S(2)}) collective-permute-start(f32[64,3,256]{2,0,1:T(8,128)S(1)} %get-tuple-element.90), channel_id=1, source_target_pairs={{0,1},{1,2},{2,3},{3,4},{4,5},{5,6},{6,7},{7,8},{8,9},{9,10},{10,1... | collective-permute-start | bytes 589832 | tf_op jit(solution)/shard_map/ppermute | solution.py:12
  234.4 12.8 %collective-permute-start.9 = (f32[64,3,256]{2,0,1:T(8,128)S(1)}, f32[64,3,256]{2,0,1:T(8,128)S(1)}, u32[]{:S(2)}, u32[]{:S(2)}) collective-permute-start(f32[64,3,256]{2,0,1:T(8,128)S(1)} %get-tuple-element.89), channel_id=1, source_target_pairs={{0,2},{1,3},{2,4},{3,5},{4,6},{5,7},{6,8},{7,9},{8,10},{9,11},{10,... | collective-permute-start | bytes 589832 | tf_op jit(solution)/shard_map/ppermute | solution.py:12
where the time goes:
time: 249 us; the launch traced here: 248 us
  other arithmetic  94.5 us (38%)
  local copies, waits for them, and re-layouts  67.2 us (27%)
  waiting for transfers between devices  44.8 us (18%)
  starting transfers between devices  38.8 us (16%)
    ppermute x10, waiting for transfers between devices, passed_along(): return lax.ppermute(value, axis, pairs)  44.8 us
    div x16, other arithmetic, pair_kernel(): (lax.erfc(dist * 0.5) + dist * (1.0 / math.sqrt(math.pi)) * jnp.exp(-r2 *...  44.4 us
    ppermute x10, starting transfers between devices, passed_along(): return lax.ppermute(value, axis, pairs)  38.8 us
    gather x16, local copies, waits for them, and re-layouts, step(): second = table[pairs[:, 1]]  37 us
    gather x16, local copies, waits for them, and re-layouts, step(): first = positions[pairs[:, 0]]  24.4 us
    reduce_sum x16, other arithmetic, pair_kernel(): on_second = -jnp.sum(weighted * first[3][None, :, None], axis=1)  19.5 us
    scatter-add x16, other arithmetic, step(): own_part = own_part.at[pairs[:, 0]].add(on_first * scale)  10.4 us
    scatter-add x16, other arithmetic, step(): react_part = react_part.at[pairs[:, 1]].add(on_second * scale)  10.4 us
  transfers between devices with their start and end apart: 10, of which 6 were waited for; matrix products, arithmetic and copies ran while one was open for 1% of the time, Pallas kernels for 0%

commit v1 on v0

v1 whole, which is shorter than its diff:
```python
import math

import jax
import jax.numpy as jnp
from jax import lax
from jax.experimental import pallas as pl
from jax.experimental.pallas import tpu as pltpu
from jax.sharding import PartitionSpec as P

F32 = jnp.float32
BF16 = jnp.bfloat16
I32 = jnp.int32
MESH = pl.DeviceIdType.MESH

SHARDS = 10
SLOTS = 8
ROWS = 8
LANES = 128
OWN = 2

SHIFT = 4.75
ERFCX = (
    -0.0001473139400949286,
    1.1441739139316924,
    4.715090554694223,
    36.5304177576356,
    -63.44030619869776,
    1227.393340985424,
    -1993.351622536244,
)
INV_SQRT_PI = 1.0 / math.sqrt(math.pi)
EXP2_SCALE = -0.25 / math.log(2.0)


def thirds(value):
    high = value.astype(BF16)
    rest = value - high.astype(F32)
    middle = rest.astype(BF16)
    low = (rest - middle.astype(F32)).astype(BF16)
    return high, middle, low


def picked(choice, value):
    total = None
    for part in reversed(thirds(value)):
        term = jnp.dot(choice, part, preferred_element_type=F32)
        total = term if total is None else total + term
    return total


def place_of(shard):
    return shard // 5, shard % 5 - 2


def neighbours(shard, sign, n_region, n_local):
    hop, offset = place_of(shard)
    region = lax.rem(lax.axis_index("region") + sign * hop + n_region, n_region)
    local = lax.rem(lax.axis_index("local") + sign * offset + n_local, n_local)
    return (region, local)


def greet(sign, n_region, n_local):
    barrier = pltpu.get_barrier_semaphore()
    for shard in range(SHARDS):
        if shard != OWN:
            pl.semaphore_signal(
                barrier,
                inc=1,
                device_id=neighbours(shard, sign, n_region, n_local),
                device_id_type=MESH,
            )
    return barrier


def push_kernel(n_region, n_local, leaves, pairs, count, msg, meta, back, over, out_msg, out_meta,
                send_sem, recv_sem, send_meta_sem, recv_meta_sem, own_sem):
    barrier = greet(-1, n_region, n_local)
    n_leaf = leaves.shape[0] // ROWS
    n_pair = pairs.shape[1]
    owner = pairs[0:1, :]
    index = pairs[1:2, :]
    shard = lax.shift_right_logical(index, 6)
    leaf = lax.bitwise_and(index, 63)
    slot = lax.broadcasted_iota(I32, (1, n_pair), 1)
    live = slot < count[0:1, 0:1]
    member = (lax.broadcasted_iota(I32, (16, n_pair), 0) == shard) & live
    member = member.astype(F32)
    before = lax.broadcasted_iota(I32, (n_pair, n_pair), 0) < lax.broadcasted_iota(I32, (n_pair, n_pair), 1)
    ahead = jnp.dot(member.astype(BF16), before.astype(F32).astype(BF16), preferred_element_type=F32)
    rank = jnp.sum(member * ahead, axis=0, keepdims=True).astype(I32)
    fits = live & (rank < SLOTS)
    seat = jnp.where(fits, shard * SLOTS + rank, -1)
    over[...] = jnp.broadcast_to(
        jnp.max(jnp.where(live & (rank >= SLOTS), 1, 0), axis=1, keepdims=True), over.shape
    )
    total = SHARDS * SLOTS
    seated = (lax.broadcasted_iota(I32, (total, n_pair), 0) == seat).astype(F32).astype(BF16)
    owned = (lax.broadcasted_iota(I32, (n_leaf, n_pair), 0) == owner).astype(F32).astype(BF16)
    last = (((1,), (1,)), ((), ()))
    choice = lax.dot_general(seated, owned, last, preferred_element_type=F32).astype(BF16)
    back[...] = lax.dot_general(owned, seated, last, preferred_element_type=F32).astype(BF16)
    named = jnp.broadcast_to((leaf + 1).astype(F32), (LANES, n_pair)).astype(BF16)
    partner = lax.dot_general(seated, named, last, preferred_element_type=F32).astype(I32) - 1
    for h in range(SHARDS):
        out_meta[h] = partner[h * SLOTS : (h + 1) * SLOTS, :]
    for row in range(ROWS):
        plane = picked(choice, leaves[pl.ds(row, n_leaf, stride=ROWS), :])
        for h in range(SHARDS):
            out_msg[h, row * SLOTS : (row + 1) * SLOTS, :] = plane[h * SLOTS : (h + 1) * SLOTS, :]

    keep_msg = pltpu.make_async_copy(out_msg.at[OWN], msg.at[OWN], own_sem.at[0])
    keep_meta = pltpu.make_async_copy(out_meta.at[OWN], meta.at[OWN], own_sem.at[1])
    keep_msg.start()
    keep_meta.start()
    pl.semaphore_wait(barrier, SHARDS - 1)
    copies = []
    for h in range(SHARDS):
        if h == OWN:
            continue
        target = neighbours(h, 1, n_region, n_local)
        for source, dest, send, recv in (
            (out_meta, meta, send_meta_sem, recv_meta_sem),
            (out_msg, msg, send_sem, recv_sem),
        ):
            copy = pltpu.make_async_remote_copy(
                src_ref=source.at[h],
                dst_ref=dest.at[h],
                send_sem=send.at[h],
                recv_sem=recv.at[h],
                device_id=target,
                device_id_type=MESH,
            )
            copy.start()
            copies.append(copy)
    for copy in copies:
        copy.wait()
    keep_msg.wait()
    keep_meta.wait()


def push(leaves, pairs, count, n_region, n_local):
    vmem = pl.BlockSpec(memory_space=pltpu.VMEM)
    anywhere = pl.BlockSpec(memory_space=pl.ANY)
    n_leaf = leaves.shape[0] // ROWS

    def kernel(*refs):
        push_kernel(n_region, n_local, *refs)

    return pl.pallas_call(
        kernel,
        out_shape=(
            jax.ShapeDtypeStruct((SHARDS, ROWS * SLOTS, LANES), F32),
            jax.ShapeDtypeStruct((SHARDS, SLOTS, LANES), I32),
            jax.ShapeDtypeStruct((n_leaf, SHARDS * SLOTS), BF16),
            jax.ShapeDtypeStruct((8, LANES), I32),
        ),
        in_specs=[vmem, vmem, vmem],
        out_specs=(anywhere, anywhere, vmem, vmem),
        scratch_shapes=[
            pltpu.VMEM((SHARDS, ROWS * SLOTS, LANES), F32),
            pltpu.VMEM((SHARDS, SLOTS, LANES), I32),
            pltpu.SemaphoreType.DMA((SHARDS,)),
            pltpu.SemaphoreType.DMA((SHARDS,)),
            pltpu.SemaphoreType.DMA((SHARDS,)),
            pltpu.SemaphoreType.DMA((SHARDS,)),
            pltpu.SemaphoreType.DMA((2,)),
        ],
        compiler_params=pltpu.CompilerParams(
            collective_id=0, has_side_effects=True, vmem_limit_bytes=32 * 2**20
        ),
        name="push",
    )(leaves, pairs, count)


def pair_strength(first, second):
    dx = second[0] - first[0]
    dy = second[1] - first[1]
    dz = second[2] - first[2]
    r2 = dx * dx + dy * dy + (dz * dz + 0.09)
    inverse = lax.rsqrt(r2)
    near = pl.reciprocal(r2 * inverse + SHIFT, approx=True)
    series = near * ERFCX[-1] + ERFCX[-2]
    for coefficient in ERFCX[-3::-1]:
        series = series * near + coefficient
    decay = jnp.exp2(r2 * EXP2_SCALE)
    return (series * inverse + INV_SQRT_PI) * ((inverse * inverse) * decay)


def weights(tile, centre):
    row = lax.broadcasted_iota(I32, (ROWS, LANES), 0)
    low = row < 4
    mass = jnp.where(
        low, jnp.broadcast_to(tile[3:4], (ROWS, LANES)), jnp.broadcast_to(tile[7:8], (ROWS, LANES))
    )
    shifted = tile - centre
    weighted = jnp.where(row % 4 == 3, mass, shifted * mass)
    a, b, c = (part.astype(F32) for part in thirds(weighted))
    a_up, b_up, c_up = (pltpu.roll(part, 4, 0) for part in (a, b, c))
    none = jnp.zeros_like(c)
    top = jnp.concatenate([jnp.where(low, a, b_up), jnp.where(low, a_up, b)], axis=1)
    bottom = jnp.concatenate([jnp.where(low, c, none), jnp.where(low, c_up, none)], axis=1)
    return shifted, jnp.concatenate([top, bottom], axis=0).astype(BF16)


def force(sums, shifted):
    top, bottom = sums[:8], sums[8:]
    joined = top + pltpu.roll(top, 4, 0) + bottom
    low = lax.broadcasted_iota(I32, (ROWS, LANES), 0) < 4
    tile = jnp.where(low, joined[:, :LANES], pltpu.roll(joined[:, LANES:], 4, 0))
    pull = jnp.where(
        low, jnp.broadcast_to(tile[3:4], (ROWS, LANES)), jnp.broadcast_to(tile[7:8], (ROWS, LANES))
    )
    return tile - shifted * pull


def pair_kernel(meta, own, msg, on_partner, on_owner, live, high, low_part, w_owner, w_partner, s_owner, s_partner):
    for ref in (on_partner, on_owner, high, low_part, w_owner, w_partner, s_owner, s_partner):
        ref[...] = jnp.zeros_like(ref)
    block = 16

    def note(slot, n):
        live[n] = slot
        return n + jnp.where(meta[slot, 0] >= 0, 1, 0)

    n_live = lax.fori_loop(0, SHARDS * SLOTS, note, jnp.int32(0))
    live[n_live] = 0

    def slot_rows(slot):
        return pl.ds(slot // SLOTS * (ROWS * SLOTS) + slot % SLOTS, ROWS, stride=SLOTS)

    def step(turn, before):
        now = live[turn]
        leaf = jnp.maximum(meta[now, 0], 0)
        here = turn % 2
        there = 1 - here
        plain = (((1,), (0,)), ((), ()))
        turned = (((1,), (1,)), ((), ()))
        wo, wp, kh, kl = w_owner[there], w_partner[there], high[there], low_part[there]
        to_partner = lax.dot_general(wo, kh, plain, preferred_element_type=F32) + lax.dot_general(
            wo, kl, plain, preferred_element_type=F32
        )
        to_owner = lax.dot_general(wp, kh, turned, preferred_element_type=F32) + lax.dot_general(
            wp, kl, turned, preferred_element_type=F32
        )
        leaf_before = jnp.maximum(meta[before, 0], 0)
        on_partner[leaf_before] = on_partner[leaf_before] + force(to_partner, s_partner[there])
        on_owner[slot_rows(before), :] = force(to_owner, s_owner[there])

        first = msg[slot_rows(now), :]
        second = own[leaf]
        low = lax.broadcasted_iota(I32, (ROWS, LANES), 0) < 4
        centre = jnp.broadcast_to(first[:, 0:1], (ROWS, LANES))
        centre = jnp.where(low, centre, pltpu.roll(centre, 4, 0))
        s_owner[here], w_owner[here] = weights(first, centre)
        s_partner[here], w_partner[here] = weights(second, centre)
        column = jnp.transpose(first)
        for half in range(2):
            for top in range(0, LANES, block):
                xi = [
                    jnp.broadcast_to(column[top : top + block, half * 4 + c : half * 4 + c + 1], (block, LANES))
                    for c in range(3)
                ]
                for side in range(2):
                    xj = [
                        jnp.broadcast_to(second[side * 4 + c : side * 4 + c + 1], (block, LANES)) for c in range(3)
                    ]
                    strength = pair_strength(xi, xj)
                    part = strength.astype(BF16)
                    rest = (strength - part.astype(F32)).astype(BF16)
                    rows = slice(half * LANES + top, half * LANES + top + block)
                    lanes = slice(side * LANES, (side + 1) * LANES)
                    high[here, rows, lanes] = part
                    low_part[here, rows, lanes] = rest
        return now

    lax.fori_loop(0, n_live + 1, step, jnp.int32(0))


def pair_forces(meta, own, msg):
    vmem = pl.BlockSpec(memory_space=pltpu.VMEM)
    width = 2 * LANES
    return pl.pallas_call(
        pair_kernel,
        out_shape=(
            jax.ShapeDtypeStruct(own.shape, F32),
            jax.ShapeDtypeStruct(msg.shape, F32),
        ),
        in_specs=[pl.BlockSpec(memory_space=pltpu.SMEM), vmem, vmem],
        out_specs=(vmem, vmem),
        scratch_shapes=[
            pltpu.SMEM((SHARDS * SLOTS + 1,), I32),
            pltpu.VMEM((2, width, width), BF16),
            pltpu.VMEM((2, width, width), BF16),
            pltpu.VMEM((2, 16, width), BF16),
            pltpu.VMEM((2, 16, width), BF16),
            pltpu.VMEM((2, ROWS, LANES), F32),
            pltpu.VMEM((2, ROWS, LANES), F32),
        ],
        compiler_params=pltpu.CompilerParams(vmem_limit_bytes=32 * 2**20),
        name="pair_forces",
    )(meta, own, msg)


def give_back_kernel(n_region, n_local, on_owner, on_partner, back, total, landed, send_sem, recv_sem, own_sem):
    barrier = greet(1, n_region, n_local)
    keep = pltpu.make_async_copy(on_owner.at[OWN], landed.at[OWN], own_sem)
    keep.start()
    pl.semaphore_wait(barrier, SHARDS - 1)
    copies = []
    for h in range(SHARDS):
        if h == OWN:
            continue
        copy = pltpu.make_async_remote_copy(
            src_ref=on_owner.at[h],
            dst_ref=landed.at[h],
            send_sem=send_sem.at[h],
            recv_sem=recv_sem.at[h],
            device_id=neighbours(h, -1, n_region, n_local),
            device_id_type=MESH,
        )
        copy.start()
        copies.append(copy)
    keep.wait()
    for copy in copies:
        copy.wait()
    choice = back[...]
    n_leaf = total.shape[1]
    for half in range(2):
        for c in range(3):
            row = half * 4 + c
            forces = jnp.concatenate(
                [landed[h, row * SLOTS : (row + 1) * SLOTS, :] for h in range(SHARDS)], axis=0
            )
            total[c, :, half * LANES : (half + 1) * LANES] = (
                picked(choice, forces) + on_partner[pl.ds(row, n_leaf, stride=ROWS), :]
            )


def give_back(on_owner, on_partner, back, n_region, n_local):
    vmem = pl.BlockSpec(memory_space=pltpu.VMEM)
    n_leaf = on_partner.shape[0] // ROWS

    def kernel(*refs):
        give_back_kernel(n_region, n_local, *refs)

    return pl.pallas_call(
        kernel,
        out_shape=jax.ShapeDtypeStruct((3, n_leaf, 2 * LANES), F32),
        in_specs=[vmem, vmem, vmem],
        out_specs=vmem,
        scratch_shapes=[
            pltpu.VMEM((SHARDS, ROWS * SLOTS, LANES), F32),
            pltpu.SemaphoreType.DMA((SHARDS,)),
            pltpu.SemaphoreType.DMA((SHARDS,)),
            pltpu.SemaphoreType.DMA,
        ],
        compiler_params=pltpu.CompilerParams(
            collective_id=1, has_side_effects=True, vmem_limit_bytes=32 * 2**20
        ),
        name="give_back",
    )(on_owner, on_partner, back)


def passed_along(value, axis, steps):
    if steps == 0:
        return value
    count = lax.axis_size(axis)
    pairs = [(source, (source + steps) % count) for source in range(count)]
    return lax.ppermute(value, axis, pairs)


def dense_pair(first, second):
    dx = second[:3, None, :] - first[:3, :, None]
    r2 = jnp.sum(dx * dx, axis=0) + 0.09
    dist = jnp.sqrt(r2)
    kern = (lax.erfc(dist * 0.5) + dist * INV_SQRT_PI * jnp.exp(-r2 * 0.25)) / (r2 * dist)
    weighted = dx * kern[None, :, :]
    on_first = jnp.sum(weighted * second[3][None, None, :], axis=2)
    on_second = -jnp.sum(weighted * first[3][None, :, None], axis=1)
    return (on_first, on_second)


def by_windows(positions, pair_list, pair_count):
    leaf_dev, _, width = positions.shape
    offsets = (-2, -1, 0, 1, 2)
    here = jnp.concatenate([passed_along(positions, "local", -offset) for offset in offsets], axis=0)
    table = jnp.concatenate([here, passed_along(here, "region", -1)], axis=0)
    span = here.shape[0]
    slots = pair_list.shape[0]
    alive = (jnp.arange(slots, dtype=I32) < pair_count[0]).astype(F32)

    def step(carry, inputs):
        own_part, react_part = carry
        pair, weight = inputs
        on_first, on_second = dense_pair(positions[pair[0]], table[pair[1]])
        own_part = own_part.at[pair[0]].add(on_first * weight)
        react_part = react_part.at[pair[1]].add(on_second * weight)
        return ((own_part, react_part), None)

    own_part = jnp.zeros((leaf_dev, 3, width), F32)
    reaction = jnp.zeros((2 * span, 3, width), F32)
    (own_part, reaction), _ = lax.scan(step, (own_part, reaction), (pair_list, alive))
    reaction = reaction[:span] + passed_along(reaction[span:], "region", 1)
    for place, offset in enumerate(offsets):
        piece = reaction[place * leaf_dev : (place + 1) * leaf_dev]
        own_part = own_part + passed_along(piece, "local", offset)
    return own_part.transpose(1, 0, 2)


def shards(positions, pair_list, pair_count, active):
    n_region = lax.axis_size("region")
    n_local = lax.axis_size("local")
    n_leaf, n_row, width = positions.shape
    leaves = positions.reshape(n_leaf, n_row, 2, LANES).transpose(0, 2, 1, 3).reshape(n_leaf * ROWS, LANES)
    msg, meta, back, over = push(leaves, pair_list.T, pair_count.reshape(1, 1), n_region, n_local)
    crowded = lax.pmax(over[0, 0], ("region", "local"))
    on_partner, on_owner = pair_forces(
        meta.reshape(SHARDS * SLOTS, LANES),
        leaves.reshape(n_leaf, ROWS, LANES),
        msg.reshape(SHARDS * ROWS * SLOTS, LANES),
    )
    total = give_back(
        on_owner.reshape(SHARDS, ROWS * SLOTS, LANES),
        on_partner.reshape(n_leaf * ROWS, LANES),
        back,
        n_region,
        n_local,
    )
    total = lax.cond(
        crowded > 0,
        lambda total: by_windows(positions, pair_list, pair_count),
        lambda total: total,
        total,
    )
    return (total * active.astype(F32)[None, :, None]).transpose(1, 0, 2)


def solution(mesh):
    return jax.shard_map(
        shards,
        mesh=mesh,
        in_specs=(
            P(("region", "local"), None, None),
            P(("region", "local"), None),
            P(("region", "local")),
            P(("region", "local")),
        ),
        out_specs=P(("region", "local"), None, None),
        check_vma=False,
    )
```

time: 249 us -> 166 us (0.67)
  the two profiles are of different devices: /device:TPU:2 before, /device:TPU:1 now
where the time goes in v1:
time: 166 us
  blocking collectives  96.2 us (58%)
  Pallas kernels  66.2 us (40%)
    pmax x1, blocking collectives, shards(): crowded = lax.pmax(over[0, 0], ('region', 'local'))  96.2 us
    pallas_call x1, Pallas kernels, pair_forces(): pl.pallas_call(pair_kernel, out_shape=(jax.ShapeDtypeStruct(own.shape, F3...  34.7 us
    pallas_call x1, Pallas kernels, push(): pl.pallas_call(kernel, out_shape=(jax.ShapeDtypeStruct((SHARDS, ROWS * SL...  19.4 us
    pallas_call x1, Pallas kernels, give_back(): pl.pallas_call(kernel, out_shape=jax.ShapeDtypeStruct((3, n_leaf, 2 * LAN...  12.2 us

profile of v1, /device:TPU:1, one launch (start us, length us, event | category | flops | bytes accessed | tf_op | source)
XLA Modules:
  0.0 165.7 jit_solution(16504065954158442149)
XLA Ops:
  0.7 19.4 %push.1 = (f32[10,64,128]{2,1,0:T(8,128)S(1)}, s32[10,8,128]{2,1,0:T(8,128)S(1)}, bf16[64,80]{1,0:T(8,128)(2,1)S(1)}, s32[8,128]{1,0:T(8,128)S(1)}) custom-call(f32[512,128]{1,0:T(8,128)} %bitcast.59, s32[2,64]{1,0:T(2,128)} %bitcast.63, s32[1,1]{1,0:T(1,128)} %bitcast.54.refs_2_), custom_call_target="tpu_custom_call" | custom-call | tf_op jit(solution)/shard_map/push/pallas_call | solution.py:149
  20.1 34.7 %pair_forces.1 = (f32[64,8,128]{2,1,0:T(8,128)S(1)}, f32[640,128]{1,0:T(8,128)S(1)}) custom-call(s32[80,128]{1,0:T(8,128)S(1)} %bitcast.58, f32[64,8,128]{2,1,0:T(8,128)} %bitcast.60, f32[640,128]{1,0:T(8,128)S(1)} %bitcast.56), custom_call_target="tpu_custom_call" | custom-call | tf_op jit(solution)/shard_map/pair_forces/pallas_call | solution.py:282
  54.7 12.2 %give_back.1 = f32[3,64,256]{2,1,0:T(8,128)S(1)} custom-call(f32[10,64,128]{2,1,0:T(8,128)S(1)} %bitcast.55, f32[512,128]{1,0:T(8,128)S(1)} %bitcast.57, bf16[64,80]{1,0:T(8,128)(2,1)S(1)} %get-tuple-element.91.refs_2_), custom_call_target="tpu_custom_call" | custom-call | tf_op jit(solution)/shard_map/give_back/pallas_call | solution.py:346
  66.9 0.5 slice.88
  67.4 96.2 %pmax.7 = s32[]{:T(128)} all-reduce(s32[]{:T(128)} %bitcast.18), channel_id=1, replica_groups=mesh['region'=16,'local'=32] {'region','local'}, use_global_device_ids=true, to_apply=%region_0.0 | all-reduce | flops 1 | bytes 8 | tf_op jit(solution)/shard_map/pmax | solution.py:416
  164.3 0.0 copy-start.4
  164.3 0.6 copy-done.4
  164.9 0.8 multiply_bitcast_fusion
  (2 shorter events, 0.0 us)
Async XLA Ops:
  164.3 0.7 copy-start.4

commit v2 on v0

v2 whole, which is shorter than its diff:
```python
import math

import jax
import jax.numpy as jnp
from jax import lax
from jax.experimental import pallas as pl
from jax.experimental.pallas import tpu as pltpu
from jax.sharding import PartitionSpec as P

F32 = jnp.float32
BF16 = jnp.bfloat16
I32 = jnp.int32
MESH = pl.DeviceIdType.MESH

SHARDS = 10
SEATS = 8
SLOTS = 7
ROWS = 8
LANES = 128
WIDTH = 2 * LANES
OWN = 2
BLOCK = 128

SHIFT = 0.25
ERFCX = (
    0.9999664993365988,
    -0.5639379807585301,
    0.10826155296772119,
    -0.0033908818915562877,
    -0.001816315565602909,
    0.00020140930421213982,
)
INV_SQRT_PI = 1.0 / math.sqrt(math.pi)
EXP2_SCALE = -0.25 / math.log(2.0)


def thirds(value):
    high = value.astype(BF16)
    rest = value - high.astype(F32)
    middle = rest.astype(BF16)
    low = (rest - middle.astype(F32)).astype(BF16)
    return high, middle, low


def picked(choice, value):
    total = None
    for part in reversed(thirds(value)):
        term = jnp.dot(choice, part, preferred_element_type=F32)
        total = term if total is None else total + term
    return total


def pair_strength(first, second):
    dx = second[0] - first[0]
    dy = second[1] - first[1]
    dz = second[2] - first[2]
    r2 = dx * dx + dy * dy + (dz * dz + 0.09)
    inverse = lax.rsqrt(r2)
    near = pl.reciprocal(inverse + SHIFT, approx=True)
    series = near * ERFCX[-1] + ERFCX[-2]
    for coefficient in ERFCX[-3::-1]:
        series = series * near + coefficient
    decay = jnp.exp2(r2 * EXP2_SCALE)
    return (series * inverse + INV_SQRT_PI) * ((inverse * inverse) * decay)


def in_halves(low_half, high_half):
    low = lax.broadcasted_iota(I32, (ROWS, LANES), 0) < 4
    return jnp.where(low, low_half, high_half)


def spread_rows(tile, row):
    return in_halves(
        jnp.broadcast_to(tile[row : row + 1], (ROWS, LANES)),
        jnp.broadcast_to(tile[row + 4 : row + 5], (ROWS, LANES)),
    )


def weights(tile, centre):
    row = lax.broadcasted_iota(I32, (ROWS, LANES), 0)
    shifted = tile - centre
    mass = spread_rows(tile, 3)
    weighted = jnp.where(row % 4 == 3, mass, shifted * mass)
    a, b, c = (part.astype(F32) for part in thirds(weighted))
    a_up, b_up, c_up = (pltpu.roll(part, 4, 0) for part in (a, b, c))
    none = jnp.zeros_like(c)
    top = jnp.concatenate([in_halves(a, b_up), in_halves(a_up, b)], axis=1)
    bottom = jnp.concatenate([in_halves(c, none), in_halves(c_up, none)], axis=1)
    return shifted, jnp.concatenate([top, bottom], axis=0).astype(BF16)


def force(sums, shifted):
    top, bottom = sums[:8], sums[8:]
    joined = top + pltpu.roll(top, 4, 0) + bottom
    tile = in_halves(joined[:, :LANES], pltpu.roll(joined[:, LANES:], 4, 0))
    return tile - shifted * spread_rows(tile, 3)


def spreader(half):
    row = lax.broadcasted_iota(I32, (32, 3 * LANES), 0)
    lane = lax.broadcasted_iota(I32, (32, 3 * LANES), 1)
    chosen = (row < 24) & (row % 8 == half * 4 + lane // LANES)
    return chosen.astype(F32).astype(BF16)


class Stage:
    shapes = (
        ((WIDTH, 3 * LANES), F32),
        ((ROWS, LANES), F32),
        ((16, WIDTH), BF16),
        ((16, WIDTH), BF16),
        ((ROWS, LANES), F32),
        ((ROWS, LANES), F32),
        ((WIDTH, WIDTH), BF16),
        ((WIDTH, WIDTH), BF16),
    )

    def __init__(self, refs):
        (self.columns, self.second, self.w_owner, self.w_partner,
         self.s_owner, self.s_partner, self.high, self.low) = refs

    def clear(self):
        for ref in (self.w_owner, self.w_partner, self.s_owner, self.s_partner, self.high, self.low):
            ref[...] = jnp.zeros_like(ref)

    def prepare(self, first, second, spread):
        corner = jnp.broadcast_to(first[:, 0:1], (ROWS, LANES))
        centre = in_halves(corner, pltpu.roll(corner, 4, 0))
        self.s_owner[...], self.w_owner[...] = weights(first, centre)
        self.s_partner[...], self.w_partner[...] = weights(second, centre)
        self.second[...] = second
        a, b, c = (part.astype(F32) for part in thirds(first))
        parts = jnp.transpose(jnp.concatenate([a, b, c, jnp.zeros_like(a)], axis=0)).astype(BF16)
        for half in range(2):
            self.columns[half * LANES : (half + 1) * LANES, :] = jnp.dot(
                parts, spread[half], preferred_element_type=F32
            )

    def strengths(self):
        second = self.second[...]
        for top in range(0, WIDTH, BLOCK):
            rows = slice(top, top + BLOCK)
            xi = [self.columns[rows, c * LANES : (c + 1) * LANES] for c in range(3)]
            for side in range(2):
                xj = [jnp.broadcast_to(second[side * 4 + c : side * 4 + c + 1], (BLOCK, LANES)) for c in range(3)]
                strength = pair_strength(xi, xj)
                part = strength.astype(BF16)
                lanes = slice(side * LANES, (side + 1) * LANES)
                self.high[rows, lanes] = part
                self.low[rows, lanes] = (strength - part.astype(F32)).astype(BF16)

    def sums(self):
        plain = (((1,), (0,)), ((), ()))
        turned = (((1,), (1,)), ((), ()))
        wo, wp, high, low = self.w_owner[...], self.w_partner[...], self.high[...], self.low[...]
        to_partner = lax.dot_general(wo, high, plain, preferred_element_type=F32) + lax.dot_general(
            wo, low, plain, preferred_element_type=F32
        )
        to_owner = lax.dot_general(wp, high, turned, preferred_element_type=F32) + lax.dot_general(
            wp, low, turned, preferred_element_type=F32
        )
        return force(to_partner, self.s_partner[...]), force(to_owner, self.s_owner[...])


def forces_kernel(n_region, n_local, leaves, pairs, count, total, over,
                  out_msg, out_meta, msg, meta, partners, named, on_partner, on_owner, landed,
                  flag_out, flag_in, spread,
                  msg_send, msg_recv, meta_send, meta_recv, back_send, back_recv, flag_send, flag_recv,
                  *stage_refs):
    here_region = lax.axis_index("region")
    here_local = lax.axis_index("local")
    n_leaf = leaves.shape[0] // ROWS
    n_pair = pairs.shape[1]
    n_seat = SHARDS * SEATS
    rounds = (n_region * n_local - 1).bit_length()
    per = len(Stage.shapes)
    stages = [Stage(stage_refs[i * per : (i + 1) * per]) for i in range(3)]
    last = (((1,), (1,)), ((), ()))

    def device(hop, offset):
        return (
            lax.rem(here_region + hop + n_region, n_region),
            lax.rem(here_local + offset + n_local, n_local),
        )

    def partner_device(h):
        return device(h // 5, h % 5 - 2)

    def lister_device(h):
        return device(-(h // 5), 2 - h % 5)

    barrier = pltpu.get_barrier_semaphore()
    friends = []
    for h in range(SHARDS):
        if h != OWN:
            friends += [(h // 5, h % 5 - 2), (-(h // 5), 2 - h % 5)]
    for step in range(rounds):
        stride = 2**step
        friend = (-(stride // n_local), -(stride % n_local))
        if friend not in friends:
            friends.append(friend)
    for friend in friends:
        pl.semaphore_signal(barrier, inc=1, device_id=device(*friend), device_id_type=MESH)

    owner = pairs[0:1, :]
    index = pairs[1:2, :]
    shard = index // 64
    leaf = index % 64
    live = lax.broadcasted_iota(I32, (1, n_pair), 1) < count[0:1, 0:1]
    member = ((lax.broadcasted_iota(I32, (16, n_pair), 0) == shard) & live).astype(F32)
    before = lax.broadcasted_iota(I32, (n_pair, n_pair), 0) < lax.broadcasted_iota(I32, (n_pair, n_pair), 1)
    ahead = jnp.dot(member.astype(BF16), before.astype(F32).astype(BF16), preferred_element_type=F32)
    rank = jnp.sum(member * ahead, axis=0, keepdims=True).astype(I32)
    seat = jnp.where(live & (rank < SLOTS), shard * SEATS + rank, -1)
    flag_out[0] = jnp.broadcast_to(
        jnp.max(jnp.where(live & (rank >= SLOTS), 1, 0), axis=1, keepdims=True), (8, LANES)
    )
    seated = (lax.broadcasted_iota(I32, (n_seat, n_pair), 0) == seat).astype(F32).astype(BF16)
    owned = (lax.broadcasted_iota(I32, (n_leaf, n_pair), 0) == owner).astype(F32).astype(BF16)
    choice = lax.dot_general(seated, owned, last, preferred_element_type=F32).astype(BF16)
    back = lax.dot_general(owned, seated, last, preferred_element_type=F32).astype(BF16)
    names = jnp.broadcast_to((leaf + 1).astype(F32), (LANES, n_pair)).astype(BF16)
    partner = lax.dot_general(seated, names, last, preferred_element_type=F32).astype(I32) - 1
    for h in range(SHARDS):
        out_meta[h] = partner[h * SEATS : (h + 1) * SEATS, :]
    for row in range(ROWS):
        plane = picked(choice, leaves[pl.ds(row, n_leaf, stride=ROWS), :])
        for h in range(SHARDS):
            out_msg[h, row * SEATS : (row + 1) * SEATS, :] = plane[h * SEATS : (h + 1) * SEATS, :]

    def message(h):
        return pltpu.make_async_remote_copy(
            src_ref=out_msg.at[h], dst_ref=msg.at[h], send_sem=msg_send.at[h], recv_sem=msg_recv.at[h],
            device_id=partner_device(h), device_id_type=MESH,
        )

    def names_of(h):
        return pltpu.make_async_remote_copy(
            src_ref=out_meta.at[h], dst_ref=meta.at[h], send_sem=meta_send.at[h], recv_sem=meta_recv.at[h],
            device_id=partner_device(h), device_id_type=MESH,
        )

    def answer(h):
        return pltpu.make_async_remote_copy(
            src_ref=on_owner.at[h], dst_ref=landed.at[h], send_sem=back_send.at[h], recv_sem=back_recv.at[h],
            device_id=lister_device(h), device_id_type=MESH,
        )

    def flag(step, stride):
        return pltpu.make_async_remote_copy(
            src_ref=flag_out.at[step], dst_ref=flag_in.at[step],
            send_sem=flag_send.at[step], recv_sem=flag_recv.at[step],
            device_id=device(stride // n_local, stride % n_local), device_id_type=MESH,
        )

    pl.semaphore_wait(barrier, len(friends))
    others = [(OWN + place) % SHARDS for place in range(1, SHARDS)]
    for h in others:
        names_of(h).start()
    for h in others:
        message(h).start()
    flag(0, 1).start()

    for half in range(2):
        spread[half] = spreader(half)
    for stage in stages:
        stage.clear()
    on_partner[...] = jnp.zeros_like(on_partner)
    on_owner[...] = jnp.zeros_like(on_owner)
    msg[OWN] = out_msg[OWN]
    meta[OWN] = out_meta[OWN]

    def gather(shards_here):
        rows = len(shards_here) * SEATS
        seats = jnp.concatenate([meta[h] for h in shards_here], axis=0)
        wanted = (seats == lax.broadcasted_iota(I32, (rows, LANES), 1)).astype(F32).astype(BF16)
        for place, h in enumerate(shards_here):
            named[h] = wanted[place * SEATS : (place + 1) * SEATS].astype(F32)
        for row in range(ROWS):
            plane = picked(wanted[:, :n_leaf], leaves[pl.ds(row, n_leaf, stride=ROWS), :])
            for place, h in enumerate(shards_here):
                partners[h, row * SEATS : (row + 1) * SEATS, :] = plane[place * SEATS : (place + 1) * SEATS, :]

    def prepare(stage, h, slot):
        seat_rows = pl.ds(slot, ROWS, stride=SEATS)
        stage.prepare(msg[h, seat_rows, :], partners[h, seat_rows, :], spread)

    def finish(stage, h, slot):
        seat_rows = pl.ds(slot, ROWS, stride=SEATS)
        on_partner[h, seat_rows, :], on_owner[h, seat_rows, :] = stage.sums()

    def stage_of(slot):
        return stages[2 if slot == SLOTS - 1 else slot % 2]

    gather([OWN])
    prepare(stage_of(0), OWN, 0)

    def turn(place, stride):
        h = lax.rem(OWN + place, SHARDS)
        h_before = lax.rem(OWN + place + SHARDS - 1, SHARDS)
        h_next = lax.rem(OWN + place + 1, SHARDS)
        finish(stage_of(SLOTS - 1), h_before, SLOTS - 1)
        stage_of(0).strengths()
        prepare(stage_of(1), h, 1)

        @pl.when(place >= 2)
        def _():
            answer(h_before).start()

        @pl.when(place == 0)
        def _():
            for other in others:
                names_of(other).wait_recv()
            gather(others)

        @pl.when(place < SHARDS - 1)
        def _():
            message(h_next).wait_recv()

        @pl.when(place < rounds)
        def _():
            flag(place, stride).wait()
            flag_out[place + 1] = jnp.maximum(flag_out[place], flag_in[place])

        @pl.when(place < rounds - 1)
        def _():
            flag(place + 1, stride * 2).start()

        for slot in range(1, SLOTS):
            finish(stage_of(slot - 1), h, slot - 1)
            stage_of(slot).strengths()
            if slot + 1 < SLOTS:
                prepare(stage_of(slot + 1), h, slot + 1)
        prepare(stage_of(0), h_next, 0)
        return stride * 2

    lax.fori_loop(0, SHARDS, turn, jnp.int32(1))
    h_end = others[-1]
    finish(stage_of(SLOTS - 1), h_end, SLOTS - 1)
    answer(h_end).start()
    over[...] = flag_out[rounds]
    for h in others:
        names_of(h).wait_send()
        message(h).wait_send()
    for h in others:
        answer(h).wait()

    wanted = jnp.concatenate([named[h] for h in range(SHARDS)], axis=0).astype(BF16)
    first = (((0,), (0,)), ((), ()))
    for half in range(2):
        for c in range(3):
            rows = slice((half * 4 + c) * SEATS, (half * 4 + c + 1) * SEATS)
            listed = jnp.concatenate(
                [(on_owner if h == OWN else landed)[h, rows, :] for h in range(SHARDS)], axis=0
            )
            met = jnp.concatenate([on_partner[h, rows, :] for h in range(SHARDS)], axis=0)
            result = None
            for part, other in zip(thirds(listed)[::-1], thirds(met)[::-1]):
                term = jnp.dot(back, part, preferred_element_type=F32) + lax.dot_general(
                    wanted, other, first, preferred_element_type=F32
                )[:n_leaf]
                result = term if result is None else result + term
            total[c, :, half * LANES : (half + 1) * LANES] = result


def forces(leaves, pairs, count, n_region, n_local):
    vmem = pl.BlockSpec(memory_space=pltpu.VMEM)
    n_leaf = leaves.shape[0] // ROWS
    rounds = (n_region * n_local - 1).bit_length()
    message = pltpu.VMEM((SHARDS, ROWS * SEATS, LANES), F32)
    names = pltpu.VMEM((SHARDS, SEATS, LANES), I32)

    def kernel(*refs):
        forces_kernel(n_region, n_local, *refs)

    return pl.pallas_call(
        kernel,
        out_shape=(
            jax.ShapeDtypeStruct((3, n_leaf, WIDTH), F32),
            jax.ShapeDtypeStruct((8, LANES), I32),
        ),
        in_specs=[vmem, vmem, vmem],
        out_specs=(vmem, vmem),
        scratch_shapes=[
            message,
            names,
            message,
            names,
            message,
            pltpu.VMEM((SHARDS, SEATS, LANES), F32),
            message,
            message,
            message,
            pltpu.VMEM((rounds + 1, 8, LANES), I32),
            pltpu.VMEM((rounds + 1, 8, LANES), I32),
            pltpu.VMEM((2, 32, 3 * LANES), BF16),
        ]
        + [pltpu.SemaphoreType.DMA((SHARDS,))] * 6
        + [pltpu.SemaphoreType.DMA((rounds,))] * 2
        + [pltpu.VMEM(*shape) for shape in Stage.shapes] * 3,
        compiler_params=pltpu.CompilerParams(
            collective_id=0, has_side_effects=True, vmem_limit_bytes=32 * 2**20
        ),
        name="forces",
    )(leaves, pairs, count)


def passed_along(value, axis, steps):
    if steps == 0:
        return value
    count = lax.axis_size(axis)
    pairs = [(source, (source + steps) % count) for source in range(count)]
    return lax.ppermute(value, axis, pairs)


def dense_pair(first, second):
    dx = second[:3, None, :] - first[:3, :, None]
    r2 = jnp.sum(dx * dx, axis=0) + 0.09
    dist = jnp.sqrt(r2)
    kern = (lax.erfc(dist * 0.5) + dist * INV_SQRT_PI * jnp.exp(-r2 * 0.25)) / (r2 * dist)
    weighted = dx * kern[None, :, :]
    on_first = jnp.sum(weighted * second[3][None, None, :], axis=2)
    on_second = -jnp.sum(weighted * first[3][None, :, None], axis=1)
    return (on_first, on_second)


def by_windows(positions, pair_list, pair_count):
    leaf_dev, _, width = positions.shape
    offsets = (-2, -1, 0, 1, 2)
    here = jnp.concatenate([passed_along(positions, "local", -offset) for offset in offsets], axis=0)
    table = jnp.concatenate([here, passed_along(here, "region", -1)], axis=0)
    span = here.shape[0]
    slots = pair_list.shape[0]
    alive = (jnp.arange(slots, dtype=I32) < pair_count[0]).astype(F32)

    def step(carry, inputs):
        own_part, react_part = carry
        pair, weight = inputs
        on_first, on_second = dense_pair(positions[pair[0]], table[pair[1]])
        own_part = own_part.at[pair[0]].add(on_first * weight)
        react_part = react_part.at[pair[1]].add(on_second * weight)
        return ((own_part, react_part), None)

    own_part = jnp.zeros((leaf_dev, 3, width), F32)
    reaction = jnp.zeros((2 * span, 3, width), F32)
    (own_part, reaction), _ = lax.scan(step, (own_part, reaction), (pair_list, alive))
    reaction = reaction[:span] + passed_along(reaction[span:], "region", 1)
    for place, offset in enumerate(offsets):
        piece = reaction[place * leaf_dev : (place + 1) * leaf_dev]
        own_part = own_part + passed_along(piece, "local", offset)
    return own_part.transpose(1, 0, 2)


def shards(positions, pair_list, pair_count, active):
    n_region = lax.axis_size("region")
    n_local = lax.axis_size("local")
    n_leaf, n_row, width = positions.shape
    leaves = positions.reshape(n_leaf, n_row, 2, LANES).transpose(0, 2, 1, 3).reshape(n_leaf * ROWS, LANES)
    total, over = forces(leaves, pair_list.T, pair_count.reshape(1, 1), n_region, n_local)
    total = lax.cond(
        over[0, 0] > 0,
        lambda total: by_windows(positions, pair_list, pair_count),
        lambda total: total,
        total,
    )
    return (total * active.astype(F32)[None, :, None]).transpose(1, 0, 2)


def solution(mesh):
    return jax.shard_map(
        shards,
        mesh=mesh,
        in_specs=(
            P(("region", "local"), None, None),
            P(("region", "local"), None),
            P(("region", "local")),
            P(("region", "local")),
        ),
        out_specs=P(("region", "local"), None, None),
        check_vma=False,
    )
```

time: 249 us -> 62.3 us (0.25)
  the two profiles are of different devices: /device:TPU:2 before, /device:TPU:8 now
where the time goes in v2:
time: 62.3 us; the launch traced here: 62.2 us
  Pallas kernels  58.9 us (95%)
  between operations  1.33 us (2%)
  local copies, waits for them, and re-layouts  1.15 us (2%)
  other arithmetic  0.76 us (1%)
    pallas_call x1, Pallas kernels, forces(): pl.pallas_call(kernel, out_shape=(jax.ShapeDtypeStruct((3, n_leaf, WIDTH)...  58.9 us

profile of v2, /device:TPU:8, one launch (start us, length us, event | category | flops | bytes accessed | tf_op | source)
XLA Modules:
  0.0 62.2 jit_solution(7318225847801124718)
XLA Ops:
  0.7 58.9 %forces.1 = (f32[3,64,256]{2,1,0:T(8,128)S(1)}, s32[8,128]{1,0:T(8,128)S(1)}) custom-call(f32[512,128]{1,0:T(8,128)} %bitcast.49, s32[2,64]{1,0:T(2,128)} %bitcast.52, s32[1,1]{1,0:T(1,128)} %bitcast.48.refs_2_), custom_call_target="tpu_custom_call" | custom-call | tf_op jit(solution)/shard_map/forces/pallas_call | solution.py:376
  59.6 0.5 slice.88
  60.7 0.0 copy-start.4
  60.8 0.6 %copy-done.4 = s32[64]{0:T(128)S(1)} copy-done((s32[64]{0:T(128)S(1)}, s32[64]{0:T(128)}, u32[]{:S(2)}) %copy-start.4) | copy-done | bytes 280
  61.4 0.8 %multiply_bitcast_fusion = f32[64,3,256]{2,0,1:T(8,128)} fusion(f32[3,64,256]{2,1,0:T(8,128)S(1)} %get-tuple-element.236, f32[64]{0:T(128)S(1)} %convert_element_type.14), kind=kLoop, calls=%fused_computation.63 | loop fusion | flops 49152 | bytes 393472 | tf_op jit(solution)/shard_map/transpose | solution.py:466
  (2 shorter events, 0.0 us)
Async XLA Ops:
  60.7 0.7 %copy-start.4 = (s32[64]{0:T(128)S(1)}, s32[64]{0:T(128)}, u32[]{:S(2)}) copy-start(s32[64]{0:T(128)} %param.15) | copy-start | bytes 772

commit v3 on v2

--- a/solution.py
+++ b/solution.py
@@ -19,7 +19,7 @@
 LANES = 128
 WIDTH = 2 * LANES
 OWN = 2
-BLOCK = 128
+BLOCK = 32
 
 SHIFT = 0.25
 ERFCX = (
@@ -31,7 +31,12 @@
     0.00020140930421213982,
 )
 INV_SQRT_PI = 1.0 / math.sqrt(math.pi)
-EXP2_SCALE = -0.25 / math.log(2.0)
+
+UNIT = math.sqrt(0.25 / math.log(2.0))
+SOFTENING = 0.09 * UNIT**2
+UNIT_SHIFT = SHIFT / UNIT
+UNIT_ERFCX = tuple(c * UNIT ** (2 - n) for n, c in enumerate(ERFCX))
+UNIT_TAIL = UNIT * INV_SQRT_PI
 
 
 def thirds(value):
@@ -54,14 +59,13 @@
     dx = second[0] - first[0]
     dy = second[1] - first[1]
     dz = second[2] - first[2]
-    r2 = dx * dx + dy * dy + (dz * dz + 0.09)
+    r2 = dx * dx + dy * dy + (dz * dz + SOFTENING)
     inverse = lax.rsqrt(r2)
-    near = pl.reciprocal(inverse + SHIFT, approx=True)
-    series = near * ERFCX[-1] + ERFCX[-2]
-    for coefficient in ERFCX[-3::-1]:
+    near = pl.reciprocal(inverse + UNIT_SHIFT, approx=True)
+    series = near * UNIT_ERFCX[-1] + UNIT_ERFCX[-2]
+    for coefficient in UNIT_ERFCX[-3::-1]:
         series = series * near + coefficient
-    decay = jnp.exp2(r2 * EXP2_SCALE)
-    return (series * inverse + INV_SQRT_PI) * ((inverse * inverse) * decay)
+    return (series * inverse + UNIT_TAIL) * pl.reciprocal(r2 * jnp.exp2(r2), approx=True)
 
 
 def in_halves(low_half, high_half):
@@ -78,7 +82,7 @@
 
 def weights(tile, centre):
     row = lax.broadcasted_iota(I32, (ROWS, LANES), 0)
-    shifted = tile - centre
+    shifted = (tile - centre) * UNIT
     mass = spread_rows(tile, 3)
     weighted = jnp.where(row % 4 == 3, mass, shifted * mass)
     a, b, c = (part.astype(F32) for part in thirds(weighted))
@@ -96,51 +100,58 @@
     return tile - shifted * spread_rows(tile, 3)
 
 
-def spreader(half):
-    row = lax.broadcasted_iota(I32, (32, 3 * LANES), 0)
-    lane = lax.broadcasted_iota(I32, (32, 3 * LANES), 1)
-    chosen = (row < 24) & (row % 8 == half * 4 + lane // LANES)
-    return chosen.astype(F32).astype(BF16)
+def flag_rounds(n_device):
+    rounds = []
+    reach = 1
+    while reach < n_device:
+        radix = min(4, n_device // reach)
+        rounds.append([reach * step for step in range(1, radix)])
+        reach *= radix
+    return rounds
 
 
 class Stage:
     shapes = (
-        ((WIDTH, 3 * LANES), F32),
-        ((ROWS, LANES), F32),
+        ((LANES, ROWS), F32),
         ((16, WIDTH), BF16),
         ((16, WIDTH), BF16),
         ((ROWS, LANES), F32),
         ((ROWS, LANES), F32),
         ((WIDTH, WIDTH), BF16),
         ((WIDTH, WIDTH), BF16),
+        ((16, WIDTH), BF16),
+        ((16, WIDTH), BF16),
+        ((ROWS, LANES), F32),
+        ((ROWS, LANES), F32),
     )
 
     def __init__(self, refs):
-        (self.columns, self.second, self.w_owner, self.w_partner,
-         self.s_owner, self.s_partner, self.high, self.low) = refs
-
-    def clear(self):
-        for ref in (self.w_owner, self.w_partner, self.s_owner, self.s_partner, self.high, self.low):
-            ref[...] = jnp.zeros_like(ref)
-
-    def prepare(self, first, second, spread):
+        (self.columns, self.w_owner, self.w_partner,
+         self.s_owner, self.s_partner, self.high, self.low,
+         self.held_w_owner, self.held_w_partner, self.held_s_owner, self.held_s_partner) = refs
+
+    def prepare(self, first, second):
         corner = jnp.broadcast_to(first[:, 0:1], (ROWS, LANES))
         centre = in_halves(corner, pltpu.roll(corner, 4, 0))
-        self.s_owner[...], self.w_owner[...] = weights(first, centre)
-        self.s_partner[...], self.w_partner[...] = weights(second, centre)
-        self.second[...] = second
-        a, b, c = (part.astype(F32) for part in thirds(first))
-        parts = jnp.transpose(jnp.concatenate([a, b, c, jnp.zeros_like(a)], axis=0)).astype(BF16)
-        for half in range(2):
-            self.columns[half * LANES : (half + 1) * LANES, :] = jnp.dot(
-                parts, spread[half], preferred_element_type=F32
-            )
+        place_first, self.w_owner[...] = weights(first, centre)
+        place_second, self.w_partner[...] = weights(second, centre)
+        self.s_owner[...] = place_first
+        self.s_partner[...] = place_second
+        self.columns[...] = jnp.transpose(place_first)
 
     def strengths(self):
-        second = self.second[...]
+        second = self.s_partner[...]
+        self.held_w_owner[...] = self.w_owner[...]
+        self.held_w_partner[...] = self.w_partner[...]
+        self.held_s_owner[...] = self.s_owner[...]
+        self.held_s_partner[...] = second
         for top in range(0, WIDTH, BLOCK):
             rows = slice(top, top + BLOCK)
-            xi = [self.columns[rows, c * LANES : (c + 1) * LANES] for c in range(3)]
+            half, top = divmod(top, LANES)
+            xi = [
+                jnp.broadcast_to(self.columns[top : top + BLOCK, at : at + 1], (BLOCK, LANES))
+                for at in range(half * 4, half * 4 + 3)
+            ]
             for side in range(2):
                 xj = [jnp.broadcast_to(second[side * 4 + c : side * 4 + c + 1], (BLOCK, LANES)) for c in range(3)]
                 strength = pair_strength(xi, xj)
@@ -152,19 +163,19 @@
     def sums(self):
         plain = (((1,), (0,)), ((), ()))
         turned = (((1,), (1,)), ((), ()))
-        wo, wp, high, low = self.w_owner[...], self.w_partner[...], self.high[...], self.low[...]
+        wo, wp, high, low = self.held_w_owner[...], self.held_w_partner[...], self.high[...], self.low[...]
         to_partner = lax.dot_general(wo, high, plain, preferred_element_type=F32) + lax.dot_general(
             wo, low, plain, preferred_element_type=F32
         )
         to_owner = lax.dot_general(wp, high, turned, preferred_element_type=F32) + lax.dot_general(
             wp, low, turned, preferred_element_type=F32
         )
-        return force(to_partner, self.s_partner[...]), force(to_owner, self.s_owner[...])
+        return force(to_partner, self.held_s_partner[...]), force(to_owner, self.held_s_owner[...])
 
 
 def forces_kernel(n_region, n_local, leaves, pairs, count, total, over,
                   out_msg, out_meta, msg, meta, partners, named, on_partner, on_owner, landed,
-                  flag_out, flag_in, spread,
+                  flag_out, flag_in, firsts, seconds, to_partners, to_owners,
                   msg_send, msg_recv, meta_send, meta_recv, back_send, back_recv, flag_send, flag_recv,
                   *stage_refs):
     here_region = lax.axis_index("region")
@@ -172,9 +183,10 @@
     n_leaf = leaves.shape[0] // ROWS
     n_pair = pairs.shape[1]
     n_seat = SHARDS * SEATS
-    rounds = (n_region * n_local - 1).bit_length()
+    rounds = flag_rounds(n_region * n_local)
+    strides = [stride for each in rounds for stride in each]
     per = len(Stage.shapes)
-    stages = [Stage(stage_refs[i * per : (i + 1) * per]) for i in range(3)]
+    stages = [Stage(stage_refs[i * per : (i + 1) * per]) for i in range(SLOTS)]
     last = (((1,), (1,)), ((), ()))
 
     def device(hop, offset):
@@ -194,8 +206,7 @@
     for h in range(SHARDS):
         if h != OWN:
             friends += [(h // 5, h % 5 - 2), (-(h // 5), 2 - h % 5)]
-    for step in range(rounds):
-        stride = 2**step
+    for stride in strides:
         friend = (-(stride // n_local), -(stride % n_local))
         if friend not in friends:
             friends.append(friend)
@@ -247,9 +258,10 @@
         )
 
     def flag(step, stride):
+        lane = strides.index(stride)
         return pltpu.make_async_remote_copy(
-            src_ref=flag_out.at[step], dst_ref=flag_in.at[step],
-            send_sem=flag_send.at[step], recv_sem=flag_recv.at[step],
+            src_ref=flag_out.at[step], dst_ref=flag_in.at[lane],
+            send_sem=flag_send.at[lane], recv_sem=flag_recv.at[lane],
             device_id=device(stride // n_local, stride % n_local), device_id_type=MESH,
         )
 
@@ -259,14 +271,11 @@
         names_of(h).start()
     for h in others:
         message(h).start()
-    flag(0, 1).start()
-
-    for half in range(2):
-        spread[half] = spreader(half)
-    for stage in stages:
-        stage.clear()
-    on_partner[...] = jnp.zeros_like(on_partner)
-    on_owner[...] = jnp.zeros_like(on_owner)
+    for stride in rounds[0]:
+        flag(0, stride).start()
+
+    to_partners[...] = jnp.zeros_like(to_partners)
+    to_owners[...] = jnp.zeros_like(to_owners)
     msg[OWN] = out_msg[OWN]
     meta[OWN] = out_meta[OWN]
 
@@ -281,64 +290,85 @@
             for place, h in enumerate(shards_here):
                 partners[h, row * SEATS : (row + 1) * SEATS, :] = plane[place * SEATS : (place + 1) * SEATS, :]
 
-    def prepare(stage, h, slot):
+    def prepare(h):
+        firsts[...] = msg[h]
+        seconds[...] = partners[h]
+
+    def prepare_slot(slot):
         seat_rows = pl.ds(slot, ROWS, stride=SEATS)
-        stage.prepare(msg[h, seat_rows, :], partners[h, seat_rows, :], spread)
-
-    def finish(stage, h, slot):
+        stages[slot].prepare(firsts[seat_rows, :], seconds[seat_rows, :])
+
+    def finish_slot(slot):
         seat_rows = pl.ds(slot, ROWS, stride=SEATS)
-        on_partner[h, seat_rows, :], on_owner[h, seat_rows, :] = stage.sums()
-
-    def stage_of(slot):
-        return stages[2 if slot == SLOTS - 1 else slot % 2]
+        to_partners[seat_rows, :], to_owners[seat_rows, :] = stages[slot].sums()
+
+    def finish(h):
+        on_partner[h] = to_partners[...]
+        on_owner[h] = to_owners[...]
+
+    turned = (here_local == 0) * 2 + (here_local == 1) * 1
+    turned = turned + (here_local == n_local - 1) * 3 + (here_local == n_local - 2) * 4
+    own_turn = 2 * ((7 - turned) % 5)
+
+    def shard_at(place):
+        turn = place + (place >= own_turn) * 1
+        return turn % 2 * 5 + 4 - (turn // 2 + turned) % 5
 
     gather([OWN])
-    prepare(stage_of(0), OWN, 0)
-
-    def turn(place, stride):
-        h = lax.rem(OWN + place, SHARDS)
-        h_before = lax.rem(OWN + place + SHARDS - 1, SHARDS)
-        h_next = lax.rem(OWN + place + 1, SHARDS)
-        finish(stage_of(SLOTS - 1), h_before, SLOTS - 1)
-        stage_of(0).strengths()
-        prepare(stage_of(1), h, 1)
+    prepare(OWN)
+    for slot in range(SLOTS):
+        prepare_slot(slot)
+    for slot in range(SLOTS):
+        stages[slot].strengths()
+    for h in others:
+        names_of(h).wait_recv()
+    gather(others)
+    first_shard = shard_at(jnp.int32(0))
+    message(first_shard).wait_recv()
+    prepare(first_shard)
+    for slot in range(SLOTS):
+        prepare_slot(slot)
+
+    def turn(place, h_before):
+        h = shard_at(place - 1)
+        h_next = shard_at(jnp.minimum(place, SHARDS - 2))
+
+        @pl.when(place < SHARDS - 1)
+        def _():
+            message(h_next).wait_recv()
+
+        for step, each in enumerate(rounds):
+
+            @pl.when(place == SHARDS - 1 - 2 * (len(rounds) - 1 - step))
+            def _(step=step, each=each):
+                heard = flag_out[step]
+                for stride in each:
+                    flag(step, stride).wait()
+                    heard = jnp.maximum(heard, flag_in[strides.index(stride)])
+                flag_out[step + 1] = heard
+                if step + 1 < len(rounds):
+                    for stride in rounds[step + 1]:
+                        flag(step + 1, stride).start()
+
+        prepare(h_next)
+        for slot in range(SLOTS):
+            finish_slot(slot)
+            stages[slot].strengths()
+            prepare_slot(slot)
+        finish(h_before)
 
         @pl.when(place >= 2)
         def _():
             answer(h_before).start()
 
-        @pl.when(place == 0)
-        def _():
-            for other in others:
-                names_of(other).wait_recv()
-            gather(others)
-
-        @pl.when(place < SHARDS - 1)
-        def _():
-            message(h_next).wait_recv()
-
-        @pl.when(place < rounds)
-        def _():
-            flag(place, stride).wait()
-            flag_out[place + 1] = jnp.maximum(flag_out[place], flag_in[place])
-
-        @pl.when(place < rounds - 1)
-        def _():
-            flag(place + 1, stride * 2).start()
-
-        for slot in range(1, SLOTS):
-            finish(stage_of(slot - 1), h, slot - 1)
-            stage_of(slot).strengths()
-            if slot + 1 < SLOTS:
-                prepare(stage_of(slot + 1), h, slot + 1)
-        prepare(stage_of(0), h_next, 0)
-        return stride * 2
-
-    lax.fori_loop(0, SHARDS, turn, jnp.int32(1))
-    h_end = others[-1]
-    finish(stage_of(SLOTS - 1), h_end, SLOTS - 1)
+        return h
+
+    h_end = lax.fori_loop(1, SHARDS, turn, jnp.int32(OWN))
+    for slot in range(SLOTS):
+        finish_slot(slot)
+    finish(h_end)
     answer(h_end).start()
-    over[...] = flag_out[rounds]
+    over[...] = flag_out[len(rounds)]
     for h in others:
         names_of(h).wait_send()
         message(h).wait_send()
@@ -366,7 +396,8 @@
 def forces(leaves, pairs, count, n_region, n_local):
     vmem = pl.BlockSpec(memory_space=pltpu.VMEM)
     n_leaf = leaves.shape[0] // ROWS
-    rounds = (n_region * n_local - 1).bit_length()
+    rounds = flag_rounds(n_region * n_local)
+    n_flag = sum(len(each) for each in rounds)
     message = pltpu.VMEM((SHARDS, ROWS * SEATS, LANES), F32)
     names = pltpu.VMEM((SHARDS, SEATS, LANES), I32)
 
@@ -391,13 +422,13 @@
             message,
             message,
             message,
-            pltpu.VMEM((rounds + 1, 8, LANES), I32),
-            pltpu.VMEM((rounds + 1, 8, LANES), I32),
-            pltpu.VMEM((2, 32, 3 * LANES), BF16),
+            pltpu.VMEM((len(rounds) + 1, 8, LANES), I32),
+            pltpu.VMEM((n_flag, 8, LANES), I32),
         ]
+        + [pltpu.VMEM((ROWS * SEATS, LANES), F32)] * 4
         + [pltpu.SemaphoreType.DMA((SHARDS,))] * 6
-        + [pltpu.SemaphoreType.DMA((rounds,))] * 2
-        + [pltpu.VMEM(*shape) for shape in Stage.shapes] * 3,
+        + [pltpu.SemaphoreType.DMA((n_flag,))] * 2
+        + [pltpu.VMEM(*shape) for shape in Stage.shapes] * SLOTS,
         compiler_params=pltpu.CompilerParams(
             collective_id=0, has_side_effects=True, vmem_limit_bytes=32 * 2**20
         ),

time: 62.3 us -> 52.4 us (0.84)
  the two profiles are of different devices: /device:TPU:8 before, /device:TPU:1 now
where the time goes in v3:
time: 52.4 us; the launch traced here: 51.4 us
  Pallas kernels  48.2 us (92%)
  between operations  1.33 us (3%)
  local copies, waits for them, and re-layouts  1.15 us (2%)
  other arithmetic  0.76 us (1%)
    pallas_call x1, Pallas kernels, forces(): pl.pallas_call(kernel, out_shape=(jax.ShapeDtypeStruct((3, n_leaf, WIDTH)...  48.2 us

profile of v3, /device:TPU:1, one launch (start us, length us, event | category | flops | bytes accessed | tf_op | source)
XLA Modules:
  0.0 51.4 jit_solution(18096567701961405649)
XLA Ops:
  0.7 48.2 %forces.1 = (f32[3,64,256]{2,1,0:T(8,128)S(1)}, s32[8,128]{1,0:T(8,128)S(1)}) custom-call(f32[512,128]{1,0:T(8,128)} %bitcast.49, s32[2,64]{1,0:T(2,128)} %bitcast.52, s32[1,1]{1,0:T(1,128)} %bitcast.48.refs_2_), custom_call_target="tpu_custom_call" | custom-call | tf_op jit(solution)/shard_map/forces/pallas_call | solution.py:407
  48.8 0.5 slice.88
  50.0 0.0 copy-start.4
  50.0 0.6 %copy-done.4 = s32[64]{0:T(128)S(1)} copy-done((s32[64]{0:T(128)S(1)}, s32[64]{0:T(128)}, u32[]{:S(2)}) %copy-start.4) | copy-done | bytes 280
  50.7 0.8 %multiply_bitcast_fusion = f32[64,3,256]{2,0,1:T(8,128)} fusion(f32[3,64,256]{2,1,0:T(8,128)S(1)} %get-tuple-element.236, f32[64]{0:T(128)S(1)} %convert_element_type.14), kind=kLoop, calls=%fused_computation.63 | loop fusion | flops 49152 | bytes 393472 | tf_op jit(solution)/shard_map/transpose | solution.py:497
  (2 shorter events, 0.0 us)
Async XLA Ops:
  50.0 0.7 %copy-start.4 = (s32[64]{0:T(128)S(1)}, s32[64]{0:T(128)}, u32[]{:S(2)}) copy-start(s32[64]{0:T(128)} %param.15) | copy-start | bytes 772

commit v4 on v3

--- a/solution.py
+++ b/solution.py
@@ -173,7 +173,7 @@
         return force(to_partner, self.held_s_partner[...]), force(to_owner, self.held_s_owner[...])
 
 
-def forces_kernel(n_region, n_local, leaves, pairs, count, total, over,
+def forces_kernel(n_region, n_local, leaves, pairs, count, active, total, over,
                   out_msg, out_meta, msg, meta, partners, named, on_partner, on_owner, landed,
                   flag_out, flag_in, firsts, seconds, to_partners, to_owners,
                   msg_send, msg_recv, meta_send, meta_recv, back_send, back_recv, flag_send, flag_recv,
@@ -230,6 +230,9 @@
     owned = (lax.broadcasted_iota(I32, (n_leaf, n_pair), 0) == owner).astype(F32).astype(BF16)
     choice = lax.dot_general(seated, owned, last, preferred_element_type=F32).astype(BF16)
     back = lax.dot_general(owned, seated, last, preferred_element_type=F32).astype(BF16)
+    square = lax.broadcasted_iota(I32, (n_leaf, n_leaf), 0) == lax.broadcasted_iota(I32, (n_leaf, n_leaf), 1)
+    kept = jnp.where(square, jnp.broadcast_to(active[...].astype(F32), (n_leaf, n_leaf)), 0.0).astype(BF16)
+    back = jnp.dot(kept, back, preferred_element_type=F32).astype(BF16)
     names = jnp.broadcast_to((leaf + 1).astype(F32), (LANES, n_pair)).astype(BF16)
     partner = lax.dot_general(seated, names, last, preferred_element_type=F32).astype(I32) - 1
     for h in range(SHARDS):
@@ -320,9 +323,15 @@
         prepare_slot(slot)
     for slot in range(SLOTS):
         stages[slot].strengths()
-    for h in others:
-        names_of(h).wait_recv()
-    gather(others)
+
+    def gather_places(group):
+        met_here = [shard_at(jnp.int32(place)) for place in group]
+        for h in met_here:
+            names_of(h).wait_recv()
+        gather(met_here)
+
+    groups = ((0, 1, 2), (3, 4, 5), (6, 7, 8))
+    gather_places(groups[0])
     first_shard = shard_at(jnp.int32(0))
     message(first_shard).wait_recv()
     prepare(first_shard)
@@ -336,6 +345,12 @@
         @pl.when(place < SHARDS - 1)
         def _():
             message(h_next).wait_recv()
+
+        for group in groups[1:]:
+
+            @pl.when(place == group[0])
+            def _(group=group):
+                gather_places(group)
 
         for step, each in enumerate(rounds):
 
@@ -372,28 +387,26 @@
     for h in others:
         names_of(h).wait_send()
         message(h).wait_send()
+
+    def planes(sources):
+        for half in range(2):
+            for c in range(3):
+                rows = slice((half * 4 + c) * SEATS, (half * 4 + c + 1) * SEATS)
+                yield c, slice(half * LANES, (half + 1) * LANES), jnp.concatenate(
+                    [source[h, rows, :] for h, source in enumerate(sources)], axis=0
+                )
+
+    wanted = jnp.concatenate([named[h] for h in range(SHARDS)], axis=0).astype(BF16)[:, :n_leaf]
+    met = lax.dot_general(kept, wanted, last, preferred_element_type=F32).astype(BF16)
+    for c, lanes, forces_met in planes([on_partner] * SHARDS):
+        total[c, :, lanes] = picked(met, forces_met)
     for h in others:
         answer(h).wait()
-
-    wanted = jnp.concatenate([named[h] for h in range(SHARDS)], axis=0).astype(BF16)
-    first = (((0,), (0,)), ((), ()))
-    for half in range(2):
-        for c in range(3):
-            rows = slice((half * 4 + c) * SEATS, (half * 4 + c + 1) * SEATS)
-            listed = jnp.concatenate(
-                [(on_owner if h == OWN else landed)[h, rows, :] for h in range(SHARDS)], axis=0
-            )
-            met = jnp.concatenate([on_partner[h, rows, :] for h in range(SHARDS)], axis=0)
-            result = None
-            for part, other in zip(thirds(listed)[::-1], thirds(met)[::-1]):
-                term = jnp.dot(back, part, preferred_element_type=F32) + lax.dot_general(
-                    wanted, other, first, preferred_element_type=F32
-                )[:n_leaf]
-                result = term if result is None else result + term
-            total[c, :, half * LANES : (half + 1) * LANES] = result
-
-
-def forces(leaves, pairs, count, n_region, n_local):
+    for c, lanes, forces_listed in planes([on_owner if h == OWN else landed for h in range(SHARDS)]):
+        total[c, :, lanes] = total[c, :, lanes] + picked(back, forces_listed)
+
+
+def forces(leaves, pairs, count, active, n_region, n_local):
     vmem = pl.BlockSpec(memory_space=pltpu.VMEM)
     n_leaf = leaves.shape[0] // ROWS
     rounds = flag_rounds(n_region * n_local)
@@ -410,7 +423,7 @@
             jax.ShapeDtypeStruct((3, n_leaf, WIDTH), F32),
             jax.ShapeDtypeStruct((8, LANES), I32),
         ),
-        in_specs=[vmem, vmem, vmem],
+        in_specs=[vmem, vmem, vmem, vmem],
         out_specs=(vmem, vmem),
         scratch_shapes=[
             message,
@@ -433,7 +446,7 @@
             collective_id=0, has_side_effects=True, vmem_limit_bytes=32 * 2**20
         ),
         name="forces",
-    )(leaves, pairs, count)
+    )(leaves, pairs, count, active)
 
 
 def passed_along(value, axis, steps):
@@ -487,14 +500,16 @@
     n_local = lax.axis_size("local")
     n_leaf, n_row, width = positions.shape
     leaves = positions.reshape(n_leaf, n_row, 2, LANES).transpose(0, 2, 1, 3).reshape(n_leaf * ROWS, LANES)
-    total, over = forces(leaves, pair_list.T, pair_count.reshape(1, 1), n_region, n_local)
+    total, over = forces(
+        leaves, pair_list.T, pair_count.reshape(1, 1), active.reshape(1, n_leaf), n_region, n_local
+    )
     total = lax.cond(
         over[0, 0] > 0,
-        lambda total: by_windows(positions, pair_list, pair_count),
+        lambda total: by_windows(positions, pair_list, pair_count) * active.astype(F32)[None, :, None],
         lambda total: total,
         total,
     )
-    return (total * active.astype(F32)[None, :, None]).transpose(1, 0, 2)
+    return total.transpose(1, 0, 2)
 
 
 def solution(mesh):

time: 52.4 us -> 52.1 us (level)
  other arithmetic: 0.76 us -> 0 us
    transpose x1 -> x0, other arithmetic: 0.76 us -> none  [shards(): return (total * active.astype(F32)[None, :, None]).transpose(1, 0, 2)]
where the time goes in v4:
time: 52.1 us; the launch traced here: 51.1 us
  Pallas kernels  48.6 us (93%)
  between operations  1.32 us (3%)
  local copies, waits for them, and re-layouts  1.19 us (2%)
    pallas_call x1, Pallas kernels, forces(): pl.pallas_call(kernel, out_shape=(jax.ShapeDtypeStruct((3, n_leaf, WIDTH)...  48.6 us

profile of v4, /device:TPU:1, one launch (start us, length us, event | category | flops | bytes accessed | tf_op | source)
XLA Modules:
  0.0 51.1 jit_solution(9676644444417019194)
XLA Ops:
  0.7 48.6 %forces.1 = (f32[3,64,256]{2,1,0:T(8,128)S(1)}, s32[8,128]{1,0:T(8,128)S(1)}) custom-call(f32[512,128]{1,0:T(8,128)} %bitcast.49, s32[2,64]{1,0:T(2,128)} %bitcast.53, s32[1,1]{1,0:T(1,128)} %bitcast.48.refs_2_, s32[1,64]{1,0:T(1,128)} %bitcast.54), custom_call_target="tpu_custom_call" | custom-call | tf_op jit(solution)/shard_map/forces/pallas_call | solution.py:420
  49.3 0.5 %slice.88 = s32[1,1]{1,0:T(1,128)} slice(s32[8,128]{1,0:T(8,128)S(1)} %get-tuple-element.85), slice={[0:1], [0:1]} | slice | bytes 8 | tf_op jit(solution)/shard_map/slice | solution.py:507
  50.5 0.7 %copy.56 = f32[64,3,256]{2,0,1:T(8,128)} copy(f32[64,3,256]{2,0,1:T(8,128)S(1)} %bitcast.50) | data formatting | bytes 393216
  (1 shorter events, 0.0 us)

commit v5 on v4

--- a/solution.py
+++ b/solution.py
@@ -104,7 +104,7 @@
     rounds = []
     reach = 1
     while reach < n_device:
-        radix = min(4, n_device // reach)
+        radix = min(8 if reach == 1 else 4, n_device // reach)
         rounds.append([reach * step for step in range(1, radix)])
         reach *= radix
     return rounds

time: 52.1 us -> 51.8 us (level)
  the two profiles are of different devices: /device:TPU:1 before, /device:TPU:65 now
where the time goes in v5:
time: 51.8 us; the launch traced here: 51.7 us
  Pallas kernels  49.2 us (95%)
  between operations  1.32 us (3%)
  local copies, waits for them, and re-layouts  1.19 us (2%)
    pallas_call x1, Pallas kernels, forces(): pl.pallas_call(kernel, out_shape=(jax.ShapeDtypeStruct((3, n_leaf, WIDTH)...  49.2 us

profile of v5, /device:TPU:65, one launch (start us, length us, event | category | flops | bytes accessed | tf_op | source)
XLA Modules:
  0.0 51.7 jit_solution(1598106222265317438)
XLA Ops:
  0.7 49.2 %forces.1 = (f32[3,64,256]{2,1,0:T(8,128)S(1)}, s32[8,128]{1,0:T(8,128)S(1)}) custom-call(f32[512,128]{1,0:T(8,128)} %bitcast.49, s32[2,64]{1,0:T(2,128)} %bitcast.53, s32[1,1]{1,0:T(1,128)} %bitcast.48.refs_2_, s32[1,64]{1,0:T(1,128)} %bitcast.54), custom_call_target="tpu_custom_call" | custom-call | tf_op jit(solution)/shard_map/forces/pallas_call | solution.py:420
  49.8 0.5 slice.88
  51.0 0.7 %copy.56 = f32[64,3,256]{2,0,1:T(8,128)} copy(f32[64,3,256]{2,0,1:T(8,128)S(1)} %bitcast.50) | data formatting | bytes 393216
  (1 shorter events, 0.0 us)
